TPU v7x, 512 devices: a whole 4x8x8 slice. The times are simulated.
512 devices in a mesh: section: 4 (over x_lo, core), seq: 64 (over z, y), batch: 2 (over x_hi).
Axes of the slice: x: 4 (x_hi: 2, x_lo: 2; x = x_hi * 2 + x_lo), y: 8, z: 8, core: 2. Of those that a mesh axis runs over, the one named last changes fastest.
Arguments:
- states: bfloat16 [4, 640, 3072], P('section', ('batch', 'seq')), parts along dimension 1, may hold values from -6 to 6
- step_index: int32 [1], replicated, may hold values from 0 to 27
- plan: int32 [29], replicated, may hold values from 0 to 1000, as said below
- time_weight: bfloat16 [3072, 256], P('seq'), may hold values from -0.375 to 0.375
- mod_weight: bfloat16 [4, 9216, 3072], P('section', 'seq'), may hold values from -0.109375 to 0.109375
- up_weight: bfloat16 [4, 12288, 3072], P('section', 'seq'), may hold values from -0.109375 to 0.109375
- down_weight: bfloat16 [4, 12288, 3072], P('section', 'seq'), may hold values from -0.0546875 to 0.0546875
Outputs:
- next_states: bfloat16 [4, 640, 3072], P('section', ('batch', 'seq')), parts along dimension 1
There are 2 independent parts, one for each index of `batch`. A program takes and returns all parts, laid end to end along the dimension named above; an argument that names none is the same for every part. Nothing has to cross between parts.
Inputs may be any that keep to these rules, and one draw needn't show every extreme that they name: `plan`: strictly decreasing, first entry 1000, last entry 0.
All inputs are finite; a program needn't handle non-finite values.
Results may differ from a plain program's by a relative error of at most 0.007.
Values may be sent and summed in bfloat16 or wider, within the bound.
A program may use at most 64 MiB of HBM per device.

v0:
```python
import math

import jax
import jax.numpy as jnp
from jax import lax
from jax.sharding import PartitionSpec as P


def shifted(value, axis, steps):
    count = lax.axis_size(axis)
    pairs = [(source, (source + steps) % count) for source in range(count)]
    return lax.ppermute(value, axis, pairs)


def by_rows(left, right):
    return lax.dot_general(
        left, right, (((1,), (1,)), ((), ())), preferred_element_type=jnp.float32
    )


def local(states, step_index, plan, time_weight, mod_weight, up_weight, down_weight):
    width = states.shape[2]
    tok_rows = states.shape[1]
    sigma = plan[step_index[0]].astype(jnp.float32) / 1000.0
    sigma_next = plan[step_index[0] + 1].astype(jnp.float32) / 1000.0
    half = time_weight.shape[1] // 2
    freqs = jnp.exp(-math.log(10000.0) * jnp.arange(half, dtype=jnp.float32) / half)
    angles = 1000.0 * sigma * freqs
    feature = jnp.concatenate([jnp.cos(angles), jnp.sin(angles)])[None, :].astype(jnp.bfloat16)
    cond_part = jax.nn.silu(by_rows(feature, time_weight)).astype(jnp.bfloat16)
    cond = lax.all_gather(cond_part, "seq", axis=1, tiled=True)
    modul_part = by_rows(cond, mod_weight[0])
    modul = lax.all_gather(modul_part, "seq", axis=1, tiled=True)
    shift, scale, gate = (modul[:, :width], modul[:, width : 2 * width], modul[:, 2 * width :])
    rows = states[0].astype(jnp.float32)
    center = rows - jnp.mean(rows, axis=-1, keepdims=True)
    spread = jnp.mean(center * center, axis=-1, keepdims=True)
    hidden = jax.nn.gelu(
        by_rows(
            lax.all_gather(
                (center * lax.rsqrt(spread + 1e-06) * (1.0 + scale) + shift).astype(jnp.bfloat16),
                "seq",
                axis=0,
                tiled=True,
            ),
            up_weight[0],
        ),
        approximate=True,
    ).astype(jnp.bfloat16)
    whole_terms = jnp.dot(hidden, down_weight[0], preferred_element_type=jnp.float32)
    summed = lax.psum(whole_terms, "seq")
    offset = lax.axis_index("seq") * tok_rows
    branch = lax.dynamic_slice_in_dim(summed, offset, tok_rows, 0)
    group_out = (rows + gate * branch).astype(jnp.bfloat16)
    section_pos = lax.axis_index("section")
    received = shifted(group_out, "section", 1)
    first = (rows + (sigma_next - sigma) * received.astype(jnp.float32)).astype(jnp.bfloat16)
    result = jnp.where(section_pos == 0, first, received)
    return result[None]


def solution(mesh):
    in_specs = (
        P("section", ("batch", "seq"), None),
        P(),
        P(),
        P("seq", None),
        P("section", "seq", None),
        P("section", "seq", None),
        P("section", "seq", None),
    )
    out_specs = P("section", ("batch", "seq"), None)
    return jax.shard_map(local, mesh=mesh, in_specs=in_specs, out_specs=out_specs, check_vma=False)
```

profile of v0, /device:TPU:1, one launch (start us, length us, event | category | flops | bytes accessed | tf_op | source)
XLA Modules:
  0.0 709.2 jit_solution(5656476594874210904)
XLA Ops:
  6.5 0.0 copy-start
  7.3 1.3 dynamic-slice
  9.7 1.4 fusion.44
  11.7 0.9 convert_reduce_fusion
  12.7 1.0 fusion.29
  13.7 0.1 sine_convert_fusion
  13.8 0.9 fusion.38
  14.6 0.3 dynamic-update-slice
  14.9 125.1 %all-reduce = bf16[3072]{0:T(1024)(128)(2,1)S(1)} all-reduce(bf16[3072]{0:T(1024)(128)(2,1)S(1)} %dynamic-update-slice), channel_id=2, replica_groups=mesh['section'=4,'seq'=64,'batch'=2] {'seq'}, use_global_device_ids=true, to_apply=%add | all-reduce | flops 3072 | bytes 12288
  140.0 1.5 fusion.4
  141.5 0.3 dynamic-update-slice.1
  141.8 219.6 %all-reduce.1 = f32[9216]{0:T(1024)S(1)} all-reduce(f32[9216]{0:T(1024)S(1)} %dynamic-update-slice.1), channel_id=3, replica_groups=mesh['section'=4,'seq'=64,'batch'=2] {'seq'}, use_global_device_ids=true, to_apply=%add.1 | all-reduce | flops 9216 | bytes 73728
  361.4 1.5 fusion.37
  362.9 0.0 all-gather.5.cloned.1.call-update
  362.9 0.0 all-reduce.4.cloned.1.call-start
  363.0 155.0 %all-gather.5.cloned.1.call-done = bf16[64,5,3072]{2,1,0:T(8,128)(2,1)} async-done(((bf16[1,5,3072]{2,1,0:T(8,128)(2,1)}), bf16[64,5,3072]{2,1,0:T(8,128)(2,1)}) %all-gather.5.cloned.1.call-update) | async-done | bytes 1966096 | tf_op jit(solution)/shard_map/all_gather | solution.py:40
  518.0 3.0 reshape.47
  521.0 5.0 fusion
  526.0 0.0 all-reduce.4.cloned.1.call-update
  526.0 166.6 %all-reduce.4.cloned.1.call-done = f32[320,3072]{1,0:T(8,128)} async-done(((f32[320,3072]{1,0:T(8,128)}), f32[320,3072]{1,0:T(8,128)}) %all-reduce.4.cloned.1.call-update) | async-done | bytes 3932176 | tf_op jit(solution)/shard_map/psum | solution.py:51
  692.6 1.0 fusion.33
  693.6 7.0 collective-permute-start
  701.2 0.5 collective-permute-done
  701.8 0.6 fusion.36
  (12 shorter events, 0.1 us)
Async XLA Ops:
  6.5 514.4 %copy-start = (bf16[1,192,3072]{2,1,0:T(8,128)(2,1)S(1)}, bf16[1,192,3072]{2,1,0:T(8,128)(2,1)}, u32[]{:S(2)}) copy-start(bf16[1,192,3072]{2,1,0:T(8,128)(2,1)} %param.13) | copy-start | bytes 3538948
  6.5 511.4 %all-gather.5.cloned.1.call-start = ((), (), s32[]{:S(2)}) async-start(), calls=%async_computation.1 | async-start | bytes 3194880 | tf_op jit(solution)/shard_map/all_gather | solution.py:40
  362.9 329.7 %all-reduce.4.cloned.1.call-start = ((), (), s32[]{:S(2)}) async-start(), calls=%async_computation | async-start | bytes 7864320 | tf_op jit(solution)/shard_map/psum | solution.py:51
  526.0 166.6 %copy-start.1 = (bf16[1,5,3072]{2,1,0:T(8,128)(2,1)S(1)}, bf16[1,5,3072]{2,1,0:T(8,128)(2,1)}, u32[]{:S(2)}) copy-start(bf16[1,5,3072]{2,1,0:T(8,128)(2,1)} %param.7) | copy-start | bytes 92164
  693.6 8.2 %collective-permute-start = (bf16[5,3072]{1,0:T(8,128)(2,1)S(1)}, bf16[5,3072]{1,0:T(8,128)(2,1)S(1)}, u32[]{:S(2)}, u32[]{:S(2)}) collective-permute-start(bf16[5,3072]{1,0:T(8,128)(2,1)S(1)} %fusion.33), channel_id=1, source_target_pairs={{0,128},{128,256},{256,384},{384,0},{1,129},{129,257},{257,385},{3... | collective-permute-start | bytes 92168 | tf_op jit(solution)/shard_map/ppermute | solution.py:12
Sparse Core Ops, SparseCore 0:
  363.0 154.8 all-gather.4
  526.1 166.4 all-reduce.3
where the time goes:
time: 710 us; the launch traced here: 709 us
  blocking collectives  345 us (49%)
  waiting for transfers between devices  322 us (45%)
  between operations  16.7 us (2%)
  matrix products  7.38 us (1%)
    unnamed x2, blocking collectives  345 us
    psum x1, waiting for transfers between devices, local(): summed = lax.psum(whole_terms, 'seq')  167 us
    all_gather x1, waiting for transfers between devices, local(): lax.all_gather((center * lax.rsqrt(spread + 1e-06) * (1.0 + scale) + shif...  155 us
  transfers between devices with their start and end apart: 3, of which 3 were waited for; matrix products, arithmetic and copies ran while one was open for 0% of the time, Pallas kernels for 0%

commit v1 on v0

v1 whole, which is shorter than its diff:
```python
import functools
import math

import jax
import jax.numpy as jnp
from jax import lax
from jax.experimental import pallas as pl
from jax.experimental.pallas import tpu as pltpu
from jax.sharding import PartitionSpec as P

MESH = pl.DeviceIdType.MESH
F32 = jnp.float32
BF16 = jnp.bfloat16
N = 8
LANES = 128
TOK = 5
CHUNKS = 24
USED = TOK * CHUNKS
ROWS = 128
PER = 48
MOD = 144
OFFSETS = (0, 1, -1, 2, -2, 3, -3, 4)


def by_rows(left, right):
    return lax.dot_general(
        left, right, (((1,), (1,)), ((), ())), preferred_element_type=F32
    )


def kernel(
    states_ref, step_ref, plan_ref, time_ref, mod_hbm, up_hbm, down_hbm,
    out_ref,
    mod_w, up_w, down_w, scaled_w, time_pad, cond_stage, cond_y, cond_z, cond_rows,
    mod_stage, mod_sum, mod_y, mod_z, shift_rows, bias_ref,
    own_f32, own, gathered, unpack, tokens, partial, pack, rs_in, final_in, final_out,
    gate_pack, raw_pack, out_send, out_recv,
    w_sem, small_send, small_recv, g_send, g_recv, rs_send, rs_recv, f_send, f_recv, s_send, s_recv,
):
    section = lax.axis_index("section")
    seq = lax.axis_index("seq")
    z, y = seq // N, lax.rem(seq, N)
    odd = lax.rem(y + z, 2)

    def at(yy, zz):
        return zz * N + yy

    def plus(v, k):
        return lax.rem(v + k + N, N)

    ring_y = [at(plus(y, k), z) for k in range(1, N)]
    ring_z = [at(y, plus(z, k)) for k in range(1, N)]
    far_first = (3, 2, 4, 1, 5, 0, 6)

    barrier = pltpu.get_barrier_semaphore()
    for q in ring_y + ring_z:
        pl.semaphore_signal(barrier, inc=1, device_id={"seq": q}, device_id_type=MESH)
    next_section = lax.rem(section + 1, 4)
    prev_section = lax.rem(section + 3, 4)
    for q in (next_section, prev_section):
        pl.semaphore_signal(barrier, inc=1, device_id={"section": q}, device_id_type=MESH)

    loads = []
    for i, (src, dst) in enumerate(((mod_hbm, mod_w), (up_hbm, up_w), (down_hbm, down_w))):
        copy = pltpu.make_async_copy(src.at[0], dst, w_sem.at[i])
        copy.start()
        loads.append(copy)

    index = step_ref[0]
    sigma = plan_ref[index].astype(F32) / 1000.0
    sigma_next = plan_ref[index + 1].astype(F32) / 1000.0
    lane = lax.broadcasted_iota(jnp.int32, (16, LANES), 1).astype(F32)
    angles = (1000.0 * sigma) * jnp.exp(lane * (-math.log(10000.0)) / LANES)
    feature = jnp.concatenate([jnp.cos(angles), jnp.sin(angles)], axis=1).astype(BF16)
    time_pad[...] = jnp.zeros_like(time_pad)
    time_pad[pl.ds(pl.multiple_of(y * PER, 16), PER), :] = time_ref[...]
    cond = by_rows(feature, time_pad[...])
    cond = (cond * jax.nn.sigmoid(cond)).astype(BF16).astype(F32)
    cond_stage[...] = jnp.zeros_like(cond_stage)
    for m in range(3):
        cond_stage[0, m : m + 1, :] = cond[0:1, m * LANES : (m + 1) * LANES]
    cond_y[y] = cond_stage[0]

    rows = states_ref[0].astype(F32)
    center = rows - jnp.mean(rows, axis=-1, keepdims=True)
    spread = jnp.mean(center * center, axis=-1, keepdims=True)
    normed = center * lax.rsqrt(spread + 1e-06)
    own_f32[USED:ROWS, :] = jnp.zeros((ROWS - USED, LANES), F32)
    raw_pack[USED:ROWS, :] = jnp.zeros((ROWS - USED, LANES), F32)
    gate_pack[USED:ROWS, :] = jnp.zeros((ROWS - USED, LANES), F32)
    for c in range(CHUNKS):
        own_f32[TOK * c : TOK * c + TOK, :] = normed[:, c * LANES : (c + 1) * LANES]
        raw_pack[TOK * c : TOK * c + TOK, :] = rows[:, c * LANES : (c + 1) * LANES]
    own[...] = own_f32[...].astype(BF16)
    for i in range(8):
        pack[i, USED:ROWS, :] = jnp.zeros((ROWS - USED, LANES), F32)

    pl.semaphore_wait(barrier, 16)

    def send(src, dst, ssem, rsem, q):
        pltpu.make_async_remote_copy(
            src_ref=src, dst_ref=dst, send_sem=ssem, recv_sem=rsem,
            device_id={"seq": q}, device_id_type=MESH,
        ).start()

    def wait(ref, sem):
        pltpu.make_async_copy(ref, ref, sem).wait()

    for k in far_first:
        send(cond_stage.at[0], cond_y.at[y], small_send.at[0], small_recv.at[0], ring_y[k])

    local = pltpu.make_async_copy(own, gathered.at[seq], g_recv.at[seq])
    local.start()
    for k in far_first:
        send(own, gathered.at[seq], g_send.at[0], g_recv.at[seq], ring_y[k] + odd * (ring_z[k] - ring_y[k]))

    wait(cond_y.at[0:7], small_recv.at[0])
    total = cond_y[0]
    for i in range(1, N):
        total = total + cond_y[i]
    cond_stage[1] = total
    cond_z[z] = total
    for k in far_first:
        send(cond_stage.at[1], cond_z.at[z], small_send.at[1], small_recv.at[1], ring_z[k])

    up_z, down_z = at(y, plus(z, 1)), at(y, plus(z, -1))
    up_y, down_y = at(plus(y, 1), z), at(plus(y, -1), z)

    def source(odd_class, offset, j):
        if odd_class:
            yy = plus(y, offset)
            return at(yy, 2 * j + lax.rem(yy + 1, 2))
        zz = plus(z, offset)
        return at(2 * j + lax.rem(zz, 2), zz)

    def forward(src, q):
        send(gathered.at[src], gathered.at[src], g_send.at[0], g_recv.at[src], q)

    def slab(offset, odd_class):
        return OFFSETS.index(offset) * 2 + odd_class

    def unpack_slab(offset, odd_class):
        s = slab(offset, odd_class)
        for j in range(4):
            unpack[j] = gathered[source(odd_class, offset, j)].astype(F32)
        for pair in range(2):
            for c in range(CHUNKS):
                both = jnp.concatenate(
                    [
                        unpack[2 * pair, TOK * c : TOK * c + 8, :],
                        unpack[2 * pair + 1, TOK * c : TOK * c + 8, :],
                    ],
                    axis=0,
                )
                tokens[s, 16 * pair : 16 * pair + 16, c * LANES : (c + 1) * LANES] = both.astype(BF16)

    def arrive(offset, odd_class, j):
        src = source(odd_class, offset, j)
        wait(gathered.at[src], g_recv.at[src])
        return src

    for j in range(4):
        for odd_class in (0, 1):
            src = arrive(0, odd_class, j)
            up, down = (up_y, down_y) if odd_class else (up_z, down_z)
            forward(src, up)
            forward(src, down)

    unpack_slab(0, 0)
    unpack_slab(0, 1)

    wait(cond_z.at[0:7], small_recv.at[1])
    for zz in range(N):
        for m in range(3):
            q = zz * 3 + m
            cond_rows[:, q * LANES : (q + 1) * LANES] = jnp.broadcast_to(
                cond_z[zz, m : m + 1, :], (16, LANES)
            ).astype(BF16)
    loads[0].wait()
    modul = by_rows(cond_rows[...], mod_w[...])[0:8]
    wide = jnp.concatenate([modul, jnp.zeros((8, N * MOD - MOD), F32)], axis=1)
    placed = jnp.zeros((8, N * MOD), F32)
    for yy in range(N):
        moved = pltpu.roll(wide, yy * MOD, 1) if yy else wide
        placed = jnp.where(y == yy, moved, placed)
    mod_stage[...] = jnp.zeros_like(mod_stage)
    for m in range(9):
        mod_stage[m : m + 1, :] = placed[0:1, m * LANES : (m + 1) * LANES]
    mod_y[y] = mod_stage[...]
    for k in far_first:
        send(mod_stage, mod_y.at[y], small_send.at[2], small_recv.at[2], ring_y[k])

    def gather_step(h):
        for j in range(4):
            for odd_class in (0, 1):
                up, down = (up_y, down_y) if odd_class else (up_z, down_z)
                src = arrive(-h, odd_class, j)
                if h < 3 or j < 2:
                    forward(src, up)
                src = arrive(h, odd_class, j)
                if h < 3 or j >= 2:
                    forward(src, down)

    def unpack_step(h):
        for odd_class in (0, 1):
            unpack_slab(h, odd_class)
            unpack_slab(-h, odd_class)

    gather_step(1)
    unpack_step(1)
    gather_step(2)

    wait(mod_y.at[0:7], small_recv.at[2])
    total = mod_y[0]
    for i in range(1, N):
        total = total + mod_y[i]
    mod_sum[...] = total
    mod_z[z] = total
    for k in far_first:
        send(mod_sum, mod_z.at[z], small_send.at[3], small_recv.at[3], ring_z[k])

    unpack_step(2)
    gather_step(3)
    unpack_step(3)
    for j in range(4):
        for odd_class in (0, 1):
            arrive(4, odd_class, j)
    unpack_slab(4, 0)
    unpack_slab(4, 1)

    wait(mod_z.at[0:7], small_recv.at[3])

    def modulation(q):
        return mod_z[q // 9, q % 9 : q % 9 + 1, :]

    loads[1].wait()
    first = lax.broadcasted_iota(jnp.int32, (16, LANES), 0)
    for c in range(CHUNKS):
        lanes = slice(c * LANES, (c + 1) * LANES)
        scale = 1.0 + modulation(CHUNKS + c)
        scaled_w[:, lanes] = (up_w[:, lanes].astype(F32) * scale).astype(BF16)
        shift = modulation(c)
        high = shift.astype(BF16).astype(F32)
        low = shift - high
        shift_rows[:, lanes] = jnp.where(first == 0, high, jnp.where(first == 1, low, 0.0)).astype(BF16)
    both = by_rows(shift_rows[...], up_w[...])
    bias_ref[...] = jnp.broadcast_to(both[0:1] + both[1:2], bias_ref.shape)
    loads[2].wait()

    def compute(first_slab, count):
        m = count * 32
        left = tokens[first_slab : first_slab + count].reshape(m, CHUNKS * LANES)
        hidden = jax.nn.gelu(by_rows(left, scaled_w[...]) + bias_ref[0:1, :], approximate=True).astype(BF16)
        for half in range(0, count * 4, 8):
            part = hidden[half * 8 : half * 8 + 64]
            for c4 in range(0, CHUNKS, 4):
                term = jnp.dot(
                    part, down_w[:, c4 * LANES : (c4 + 4) * LANES], preferred_element_type=F32
                )
                for i in range(8):
                    for c in range(4):
                        r = TOK * (c4 + c)
                        pack[i, r : r + TOK, :] = term[8 * i : 8 * i + TOK, c * LANES : (c + 1) * LANES]
            for i in range(8):
                b = half + i
                partial[first_slab + b // 4, b % 4] = pack[i].astype(BF16)

    towards = (up_z, down_z, up_y, down_y)

    def rs_send_to(direction, step, j):
        k = 5 - step
        offset = k if direction % 2 == 0 or k == 4 else -k
        send(
            partial.at[slab(offset, direction // 2), j], rs_in.at[direction, step - 1, j],
            rs_send.at[0], rs_recv.at[direction, step - 1, j], towards[direction],
        )

    def rs_add(direction, step, j):
        k = 5 - step
        offset = k if direction % 2 == 0 else -k
        ref = rs_in.at[direction, step - 2, j]
        wait(ref, rs_recv.at[direction, step - 2, j])
        s = slab(offset, direction // 2)
        partial[s, j] = (partial[s, j].astype(F32) + ref[...].astype(F32)).astype(BF16)

    def halves(direction):
        return (0, 1) if direction % 2 == 0 else (2, 3)

    compute(14, 2)
    for i in range(2):
        for direction in range(4):
            rs_send_to(direction, 1, halves(direction)[i])
    compute(10, 4)
    for i in range(2):
        for direction in range(4):
            rs_send_to(direction, 2, halves(direction + 1)[i])
    for i in range(2):
        for direction in range(4):
            j = halves(direction)[i]
            rs_add(direction, 2, j)
            rs_send_to(direction, 2, j)
    compute(6, 4)
    for step in (3, 4):
        for j in (2, 3, 0, 1):
            for direction in range(4):
                jj = j if direction % 2 == 0 else 3 - j
                rs_add(direction, step, jj)
                rs_send_to(direction, step, jj)
        if step == 3:
            compute(2, 4)
    compute(0, 2)

    for c in range(CHUNKS):
        gate_pack[TOK * c : TOK * c + TOK, :] = jnp.broadcast_to(modulation(2 * CHUNKS + c), (TOK, LANES))

    for j in (2, 3, 0, 1):
        for odd_class in (0, 1):
            value = partial[slab(0, odd_class), j].astype(F32)
            for direction in (2 * odd_class, 2 * odd_class + 1):
                ref = rs_in.at[direction, 3, j]
                wait(ref, rs_recv.at[direction, 3, j])
                value = value + ref[...].astype(F32)
            final_out[odd_class, j] = value.astype(BF16)
            target = source(odd_class, 0, j)
            mine = z if odd_class else y

            @pl.when(target != seq)
            def _(odd_class=odd_class, j=j, target=target, mine=mine):
                send(final_out.at[odd_class, j], final_in.at[mine], f_send.at[0], f_recv.at[0], target)

            @pl.when(target == seq)
            def _(odd_class=odd_class, j=j, mine=mine):
                pltpu.make_async_copy(final_out.at[odd_class, j], final_in.at[mine], f_recv.at[0]).start()

    wait(final_in, f_recv.at[0])
    branch = final_in[0].astype(F32)
    for i in range(1, N):
        branch = branch + final_in[i].astype(F32)
    out_send[...] = (raw_pack[...] + gate_pack[...] * branch).astype(BF16)
    shift_copy = pltpu.make_async_remote_copy(
        src_ref=out_send, dst_ref=out_recv, send_sem=s_send.at[0], recv_sem=s_recv.at[0],
        device_id={"section": next_section}, device_id_type=MESH,
    )
    shift_copy.start()

    for i, ref in enumerate((cond_y, cond_z, mod_y, mod_z)):
        wait(ref.at[0:7], small_send.at[i])
    wait(gathered.at[0:63], g_send.at[0])
    wait(partial.at[0:14], rs_send.at[0])
    wait(final_in.at[0:7], f_send.at[0])
    shift_copy.wait()

    received = out_recv[...].astype(F32)
    moved = raw_pack[...] + (sigma_next - sigma) * received
    own_f32[...] = jnp.where(section == 0, moved, received)
    for c in range(CHUNKS):
        out_ref[0, :, c * LANES : (c + 1) * LANES] = own_f32[TOK * c : TOK * c + TOK, :].astype(BF16)


def local(states, step_index, plan, time_weight, mod_weight, up_weight, down_weight):
    vmem = pl.BlockSpec(memory_space=pltpu.VMEM)
    smem = pl.BlockSpec(memory_space=pltpu.SMEM)
    anywhere = pl.BlockSpec(memory_space=pl.ANY)
    dma = pltpu.SemaphoreType.DMA
    width = states.shape[2]
    hidden = up_weight.shape[1]
    block = (ROWS, LANES)
    return pl.pallas_call(
        kernel,
        out_shape=jax.ShapeDtypeStruct(states.shape, states.dtype),
        in_specs=[vmem, smem, smem, vmem, anywhere, anywhere, anywhere],
        out_specs=vmem,
        scratch_shapes=[
            pltpu.VMEM((MOD, width), BF16),
            pltpu.VMEM((hidden, width), BF16),
            pltpu.VMEM((hidden, width), BF16),
            pltpu.VMEM((hidden, width), BF16),
            pltpu.VMEM((N * PER, 256), BF16),
            pltpu.VMEM((2, 8, LANES), F32),
            pltpu.VMEM((N, 8, LANES), F32),
            pltpu.VMEM((N, 8, LANES), F32),
            pltpu.VMEM((16, width), BF16),
            pltpu.VMEM((16, LANES), F32),
            pltpu.VMEM((16, LANES), F32),
            pltpu.VMEM((N, 16, LANES), F32),
            pltpu.VMEM((N, 16, LANES), F32),
            pltpu.VMEM((16, width), BF16),
            pltpu.VMEM((8, hidden), F32),
            pltpu.VMEM(block, F32),
            pltpu.VMEM(block, BF16),
            pltpu.VMEM((64,) + block, BF16),
            pltpu.VMEM((4,) + block, F32),
            pltpu.VMEM((16, 32, width), BF16),
            pltpu.VMEM((16, 4) + block, BF16),
            pltpu.VMEM((8,) + block, F32),
            pltpu.VMEM((4, 4, 4) + block, BF16),
            pltpu.VMEM((N,) + block, BF16),
            pltpu.VMEM((2, 4) + block, BF16),
            pltpu.VMEM(block, F32),
            pltpu.VMEM(block, F32),
            pltpu.VMEM(block, BF16),
            pltpu.VMEM(block, BF16),
            dma((3,)), dma((4,)), dma((4,)), dma((1,)), dma((64,)),
            dma((1,)), dma((4, 4, 4)), dma((1,)), dma((1,)), dma((1,)), dma((1,)),
        ],
        name="denoise",
        cost_estimate=pl.CostEstimate(flops=800_000_000, bytes_accessed=3_300_000, transcendentals=100_000),
        compiler_params=pltpu.CompilerParams(
            collective_id=0, has_side_effects=True, vmem_limit_bytes=40 * 1024 * 1024
        ),
    )(states, step_index, plan, time_weight, mod_weight, up_weight, down_weight)


def solution(mesh):
    in_specs = (
        P("section", ("batch", "seq"), None),
        P(),
        P(),
        P("seq", None),
        P("section", "seq", None),
        P("section", "seq", None),
        P("section", "seq", None),
    )
    out_specs = P("section", ("batch", "seq"), None)
    return jax.shard_map(local, mesh=mesh, in_specs=in_specs, out_specs=out_specs, check_vma=False)
```

time: 710 us -> 71.9 us (0.10)
  blocking collectives: 345 us -> 0 us
  waiting for transfers between devices: 322 us -> 0 us
  Pallas kernels: 0 us -> 64.3 us
  between operations: 16.7 us -> 0.67 us
  matrix products: 7.38 us -> 0 us
    unnamed x2 -> x0, blocking collectives: 345 us -> none
    psum x1 -> x0, waiting for transfers between devices: 167 us -> none  [local(): summed = lax.psum(whole_terms, 'seq')]
    all_gather x1 -> x0, waiting for transfers between devices: 155 us -> none  [local(): lax.all_gather((center * lax.rsqrt(spread + 1e-06) * (1.0 + scale) + shif...]
    pallas_call x0 -> x1, Pallas kernels: none -> 64.3 us  [local(): pl.pallas_call(kernel, out_shape=jax.ShapeDtypeStruct(states.shape, state...]
    dot_general x3 -> x0, matrix products: 7.38 us -> none  [the longest x1 5.02 us: local(): jnp.dot(hidden, down_weight[0], preferred_element_type=jnp.float32)]
  transfers between devices with their start and end apart: 3 -> 0, of which waited for: 3 -> 0; matrix products, arithmetic and copies ran while one was open for 0% -> 0% of each run, Pallas kernels for 0% -> 0%
where the time goes in v1:
time: 71.9 us; the launch traced here: 71.5 us
  Pallas kernels  64.3 us (89%)
  local copies, waits for them, and re-layouts  6.51 us (9%)
    pallas_call x1, Pallas kernels, local(): pl.pallas_call(kernel, out_shape=jax.ShapeDtypeStruct(states.shape, state...  64.3 us
    unnamed x13, local copies, waits for them, and re-layouts  6.51 us

profile of v1, /device:TPU:1, one launch (start us, length us, event | category | flops | bytes accessed | tf_op | source)
XLA Modules:
  0.0 71.5 jit_solution(13926273002270192219)
XLA Ops:
  0.7 0.0 copy-start
  0.7 1.3 %copy-done = bf16[1,192,3072]{2,1,0:T(8,128)(2,1)S(1)} copy-done((bf16[1,192,3072]{2,1,0:T(8,128)(2,1)S(1)}, bf16[1,192,3072]{2,1,0:T(8,128)(2,1)}, u32[]{:S(2)}) %copy-start) | copy-done | bytes 1179672
  1.9 0.0 copy-start.1
  1.9 1.3 %copy-done.1 = bf16[1,192,3072]{2,1,0:T(8,128)(2,1)S(1)} copy-done((bf16[1,192,3072]{2,1,0:T(8,128)(2,1)S(1)}, bf16[1,192,3072]{2,1,0:T(8,128)(2,1)}, u32[]{:S(2)}) %copy-start.1) | copy-done | bytes 1179672
  3.2 0.0 copy-start.2
  3.2 1.2 %copy-done.2 = bf16[1,144,3072]{2,1,0:T(8,128)(2,1)S(1)} copy-done((bf16[1,144,3072]{2,1,0:T(8,128)(2,1)S(1)}, bf16[1,144,3072]{2,1,0:T(8,128)(2,1)}, u32[]{:S(2)}) %copy-start.2) | copy-done | bytes 884760
  4.4 0.0 copy-start.3
  4.4 0.8 %copy-done.3 = bf16[1,5,3072]{2,1,0:T(8,128)(2,1)S(1)} copy-done((bf16[1,5,3072]{2,1,0:T(8,128)(2,1)S(1)}, bf16[1,5,3072]{2,1,0:T(8,128)(2,1)}, u32[]{:S(2)}) %copy-start.3) | copy-done | bytes 30744
  5.2 0.0 copy-start.4
  5.2 0.7 %copy-done.4 = bf16[48,256]{1,0:T(8,128)(2,1)S(1)} copy-done((bf16[48,256]{1,0:T(8,128)(2,1)S(1)}, bf16[48,256]{1,0:T(8,128)(2,1)}, u32[]{:S(2)}) %copy-start.4) | copy-done | bytes 24600
  5.9 0.0 copy-start.5
  5.9 0.7 copy-done.5
  6.6 64.3 %denoise.1 = bf16[1,5,3072]{2,1,0:T(8,128)(2,1)S(1)} custom-call(bf16[1,5,3072]{2,1,0:T(8,128)(2,1)S(1)} %copy-done.3, s32[1]{0:T(128)S(6)} %copy.9.step_ref, s32[29]{0:T(128)S(1)} %copy-done.5, bf16[48,256]{1,0:T(8,128)(2,1)S(1)} %copy-done.4, bf16[1,144,3072]{2,1,0:T(8,128)(2,1)S(1)} %copy-done.2, bf16[1,192,3072]{2,1,0:T(8,128)(2,1)S(1)} %copy-done, ...), custom_call_target="tpu_custom_call" | custom-call | flops 800000000 | bytes 3300000 | tf_op jit(solution)/shard_map/denoise/pallas_call | solution.py:368
  70.9 0.6 copy.10
Async XLA Ops:
  0.7 1.3 %copy-start = (bf16[1,192,3072]{2,1,0:T(8,128)(2,1)S(1)}, bf16[1,192,3072]{2,1,0:T(8,128)(2,1)}, u32[]{:S(2)}) copy-start(bf16[1,192,3072]{2,1,0:T(8,128)(2,1)} %up_hbm.1) | copy-start | bytes 3538948
  1.9 1.3 %copy-start.1 = (bf16[1,192,3072]{2,1,0:T(8,128)(2,1)S(1)}, bf16[1,192,3072]{2,1,0:T(8,128)(2,1)}, u32[]{:S(2)}) copy-start(bf16[1,192,3072]{2,1,0:T(8,128)(2,1)} %down_hbm.1) | copy-start | bytes 3538948
  3.2 1.2 %copy-start.2 = (bf16[1,144,3072]{2,1,0:T(8,128)(2,1)S(1)}, bf16[1,144,3072]{2,1,0:T(8,128)(2,1)}, u32[]{:S(2)}) copy-start(bf16[1,144,3072]{2,1,0:T(8,128)(2,1)} %mod_hbm.1) | copy-start | bytes 2654212
  4.4 0.8 %copy-start.3 = (bf16[1,5,3072]{2,1,0:T(8,128)(2,1)S(1)}, bf16[1,5,3072]{2,1,0:T(8,128)(2,1)}, u32[]{:S(2)}) copy-start(bf16[1,5,3072]{2,1,0:T(8,128)(2,1)} %states_ref.1) | copy-start | bytes 92164
  5.2 0.7 %copy-start.4 = (bf16[48,256]{1,0:T(8,128)(2,1)S(1)}, bf16[48,256]{1,0:T(8,128)(2,1)}, u32[]{:S(2)}) copy-start(bf16[48,256]{1,0:T(8,128)(2,1)} %time_ref.1) | copy-start | bytes 73732
  5.9 0.7 copy-start.5

commit v2 on v1

--- a/solution.py
+++ b/solution.py
@@ -19,6 +19,9 @@
 ROWS = 128
 PER = 48
 MOD = 144
+EVERYONE = sorted(
+    ((dy, dz) for dy in range(-3, 5) for dz in range(-3, 5) if dy or dz), key=lambda d: (-abs(d[0]) - abs(d[1]), d)
+)
 OFFSETS = (0, 1, -1, 2, -2, 3, -3, 4)
 
 
@@ -29,13 +32,14 @@
 
 
 def kernel(
-    states_ref, step_ref, plan_ref, time_ref, mod_hbm, up_hbm, down_hbm,
+    states_hbm, step_hbm, plan_hbm, time_hbm, mod_hbm, up_hbm, down_hbm,
     out_ref,
+    states_ref, step_ref, plan_ref, time_ref,
     mod_w, up_w, down_w, scaled_w, time_pad, cond_stage, cond_y, cond_z, cond_rows,
-    mod_stage, mod_sum, mod_y, mod_z, shift_rows, bias_ref,
+    mod_stage, mod_all, shift_rows, bias_ref,
     own_f32, own, gathered, unpack, tokens, partial, pack, rs_in, final_in, final_out,
-    gate_pack, raw_pack, out_send, out_recv,
-    w_sem, small_send, small_recv, g_send, g_recv, rs_send, rs_recv, f_send, f_recv, s_send, s_recv,
+    gate_pack, raw_pack, own_rows, rows_in, gate_out, gate_in,
+    w_sem, small_send, small_recv, g_send, g_recv, rs_send, rs_recv, f_send, f_recv, s_send, s_recv, ready,
 ):
     section = lax.axis_index("section")
     seq = lax.axis_index("seq")
@@ -61,11 +65,15 @@
         pl.semaphore_signal(barrier, inc=1, device_id={"section": q}, device_id_type=MESH)
 
     loads = []
-    for i, (src, dst) in enumerate(((mod_hbm, mod_w), (up_hbm, up_w), (down_hbm, down_w))):
-        copy = pltpu.make_async_copy(src.at[0], dst, w_sem.at[i])
+    sources = (step_hbm, plan_hbm, time_hbm, states_hbm, mod_hbm.at[0], up_hbm.at[0], down_hbm.at[0])
+    targets = (step_ref, plan_ref, time_ref, states_ref, mod_w, up_w, down_w)
+    for i, (src, dst) in enumerate(zip(sources, targets)):
+        copy = pltpu.make_async_copy(src, dst, w_sem.at[i])
         copy.start()
         loads.append(copy)
 
+    loads[0].wait()
+    loads[1].wait()
     index = step_ref[0]
     sigma = plan_ref[index].astype(F32) / 1000.0
     sigma_next = plan_ref[index + 1].astype(F32) / 1000.0
@@ -73,6 +81,7 @@
     angles = (1000.0 * sigma) * jnp.exp(lane * (-math.log(10000.0)) / LANES)
     feature = jnp.concatenate([jnp.cos(angles), jnp.sin(angles)], axis=1).astype(BF16)
     time_pad[...] = jnp.zeros_like(time_pad)
+    loads[2].wait()
     time_pad[pl.ds(pl.multiple_of(y * PER, 16), PER), :] = time_ref[...]
     cond = by_rows(feature, time_pad[...])
     cond = (cond * jax.nn.sigmoid(cond)).astype(BF16).astype(F32)
@@ -81,6 +90,7 @@
         cond_stage[0, m : m + 1, :] = cond[0:1, m * LANES : (m + 1) * LANES]
     cond_y[y] = cond_stage[0]
 
+    loads[3].wait()
     rows = states_ref[0].astype(F32)
     center = rows - jnp.mean(rows, axis=-1, keepdims=True)
     spread = jnp.mean(center * center, axis=-1, keepdims=True)
@@ -92,10 +102,12 @@
         own_f32[TOK * c : TOK * c + TOK, :] = normed[:, c * LANES : (c + 1) * LANES]
         raw_pack[TOK * c : TOK * c + TOK, :] = rows[:, c * LANES : (c + 1) * LANES]
     own[...] = own_f32[...].astype(BF16)
+    own_rows[...] = raw_pack[...].astype(BF16)
     for i in range(8):
         pack[i, USED:ROWS, :] = jnp.zeros((ROWS - USED, LANES), F32)
 
     pl.semaphore_wait(barrier, 16)
+    pl.semaphore_signal(ready, inc=1, device_id={"section": prev_section}, device_id_type=MESH)
 
     def send(src, dst, ssem, rsem, q):
         pltpu.make_async_remote_copy(
@@ -106,6 +118,12 @@
     def wait(ref, sem):
         pltpu.make_async_copy(ref, ref, sem).wait()
 
+    def pass_on(src, dst, ssem, rsem, q):
+        return pltpu.make_async_remote_copy(
+            src_ref=src, dst_ref=dst, send_sem=ssem, recv_sem=rsem,
+            device_id={"section": next_section, "seq": q}, device_id_type=MESH,
+        )
+
     for k in far_first:
         send(cond_stage.at[0], cond_y.at[y], small_send.at[0], small_recv.at[0], ring_y[k])
 
@@ -113,6 +131,9 @@
     local.start()
     for k in far_first:
         send(own, gathered.at[seq], g_send.at[0], g_recv.at[seq], ring_y[k] + odd * (ring_z[k] - ring_y[k]))
+
+    rows_copy = pass_on(own_rows, rows_in, s_send.at[0], s_recv.at[0], seq)
+    rows_copy.start()
 
     wait(cond_y.at[0:7], small_recv.at[0])
     total = cond_y[0]
@@ -176,19 +197,17 @@
             cond_rows[:, q * LANES : (q + 1) * LANES] = jnp.broadcast_to(
                 cond_z[zz, m : m + 1, :], (16, LANES)
             ).astype(BF16)
-    loads[0].wait()
+    loads[4].wait()
     modul = by_rows(cond_rows[...], mod_w[...])[0:8]
-    wide = jnp.concatenate([modul, jnp.zeros((8, N * MOD - MOD), F32)], axis=1)
-    placed = jnp.zeros((8, N * MOD), F32)
-    for yy in range(N):
-        moved = pltpu.roll(wide, yy * MOD, 1) if yy else wide
-        placed = jnp.where(y == yy, moved, placed)
-    mod_stage[...] = jnp.zeros_like(mod_stage)
-    for m in range(9):
-        mod_stage[m : m + 1, :] = placed[0:1, m * LANES : (m + 1) * LANES]
-    mod_y[y] = mod_stage[...]
-    for k in far_first:
-        send(mod_stage, mod_y.at[y], small_send.at[2], small_recv.at[2], ring_y[k])
+    wide = jnp.concatenate([modul, jnp.zeros((8, 2 * LANES - MOD), F32)], axis=1)
+    placed = wide
+    for yy in range(1, N):
+        placed = jnp.where(y == yy, pltpu.roll(wide, yy * (MOD - LANES), 1), placed)
+    for m in range(2):
+        mod_stage[0, m : m + 1, :] = placed[0:1, m * LANES : (m + 1) * LANES]
+    mod_all[seq] = mod_stage[0]
+    for dy, dz in EVERYONE:
+        send(mod_stage.at[0], mod_all.at[seq], small_send.at[2], small_recv.at[2], at(plus(y, dy), plus(z, dz)))
 
     def gather_step(h):
         for j in range(4):
@@ -210,15 +229,6 @@
     unpack_step(1)
     gather_step(2)
 
-    wait(mod_y.at[0:7], small_recv.at[2])
-    total = mod_y[0]
-    for i in range(1, N):
-        total = total + mod_y[i]
-    mod_sum[...] = total
-    mod_z[z] = total
-    for k in far_first:
-        send(mod_sum, mod_z.at[z], small_send.at[3], small_recv.at[3], ring_z[k])
-
     unpack_step(2)
     gather_step(3)
     unpack_step(3)
@@ -228,12 +238,18 @@
     unpack_slab(4, 0)
     unpack_slab(4, 1)
 
-    wait(mod_z.at[0:7], small_recv.at[3])
+    wait(mod_all.at[0:63], small_recv.at[2])
 
     def modulation(q):
-        return mod_z[q // 9, q % 9 : q % 9 + 1, :]
-
-    loads[1].wait()
+        block, m = q // 9 * N, q % 9
+        value = jnp.zeros((1, LANES), F32)
+        if m < N:
+            value = value + mod_all[block + m, 0:1, :]
+        if m:
+            value = value + mod_all[block + m - 1, 1:2, :]
+        return value
+
+    loads[5].wait()
     first = lax.broadcasted_iota(jnp.int32, (16, LANES), 0)
     for c in range(CHUNKS):
         lanes = slice(c * LANES, (c + 1) * LANES)
@@ -245,7 +261,12 @@
         shift_rows[:, lanes] = jnp.where(first == 0, high, jnp.where(first == 1, low, 0.0)).astype(BF16)
     both = by_rows(shift_rows[...], up_w[...])
     bias_ref[...] = jnp.broadcast_to(both[0:1] + both[1:2], bias_ref.shape)
-    loads[2].wait()
+    loads[6].wait()
+
+    for c in range(CHUNKS):
+        gate_out[c : c + 1, :] = modulation(2 * CHUNKS + c)
+    gate_copy = pass_on(gate_out, gate_in, s_send.at[1], s_recv.at[1], seq)
+    gate_copy.start()
 
     def compute(first_slab, count):
         m = count * 32
@@ -310,8 +331,10 @@
             compute(2, 4)
     compute(0, 2)
 
+    wait(gate_in, s_recv.at[1])
     for c in range(CHUNKS):
-        gate_pack[TOK * c : TOK * c + TOK, :] = jnp.broadcast_to(modulation(2 * CHUNKS + c), (TOK, LANES))
+        gate_pack[TOK * c : TOK * c + TOK, :] = jnp.broadcast_to(gate_in[c : c + 1, :], (TOK, LANES))
+    pl.semaphore_wait(ready, 1)
 
     for j in (2, 3, 0, 1):
         for odd_class in (0, 1):
@@ -321,45 +344,33 @@
                 wait(ref, rs_recv.at[direction, 3, j])
                 value = value + ref[...].astype(F32)
             final_out[odd_class, j] = value.astype(BF16)
-            target = source(odd_class, 0, j)
-            mine = z if odd_class else y
-
-            @pl.when(target != seq)
-            def _(odd_class=odd_class, j=j, target=target, mine=mine):
-                send(final_out.at[odd_class, j], final_in.at[mine], f_send.at[0], f_recv.at[0], target)
-
-            @pl.when(target == seq)
-            def _(odd_class=odd_class, j=j, mine=mine):
-                pltpu.make_async_copy(final_out.at[odd_class, j], final_in.at[mine], f_recv.at[0]).start()
+            pass_on(
+                final_out.at[odd_class, j], final_in.at[z if odd_class else y], f_send.at[0], f_recv.at[0],
+                source(odd_class, 0, j),
+            ).start()
 
     wait(final_in, f_recv.at[0])
     branch = final_in[0].astype(F32)
     for i in range(1, N):
         branch = branch + final_in[i].astype(F32)
-    out_send[...] = (raw_pack[...] + gate_pack[...] * branch).astype(BF16)
-    shift_copy = pltpu.make_async_remote_copy(
-        src_ref=out_send, dst_ref=out_recv, send_sem=s_send.at[0], recv_sem=s_recv.at[0],
-        device_id={"section": next_section}, device_id_type=MESH,
-    )
-    shift_copy.start()
-
-    for i, ref in enumerate((cond_y, cond_z, mod_y, mod_z)):
-        wait(ref.at[0:7], small_send.at[i])
-    wait(gathered.at[0:63], g_send.at[0])
-    wait(partial.at[0:14], rs_send.at[0])
-    wait(final_in.at[0:7], f_send.at[0])
-    shift_copy.wait()
-
-    received = out_recv[...].astype(F32)
+    wait(rows_in, s_recv.at[0])
+    received = (rows_in[...].astype(F32) + gate_pack[...] * branch).astype(BF16).astype(F32)
     moved = raw_pack[...] + (sigma_next - sigma) * received
     own_f32[...] = jnp.where(section == 0, moved, received)
     for c in range(CHUNKS):
         out_ref[0, :, c * LANES : (c + 1) * LANES] = own_f32[TOK * c : TOK * c + TOK, :].astype(BF16)
 
+    for i, ref in enumerate((cond_y.at[0:7], cond_z.at[0:7], mod_all.at[0:63])):
+        wait(ref, small_send.at[i])
+    wait(gathered.at[0:63], g_send.at[0])
+    wait(partial.at[0:14], rs_send.at[0])
+    wait(final_in, f_send.at[0])
+    rows_copy.wait_send()
+    gate_copy.wait_send()
+
 
 def local(states, step_index, plan, time_weight, mod_weight, up_weight, down_weight):
     vmem = pl.BlockSpec(memory_space=pltpu.VMEM)
-    smem = pl.BlockSpec(memory_space=pltpu.SMEM)
     anywhere = pl.BlockSpec(memory_space=pl.ANY)
     dma = pltpu.SemaphoreType.DMA
     width = states.shape[2]
@@ -368,9 +379,13 @@
     return pl.pallas_call(
         kernel,
         out_shape=jax.ShapeDtypeStruct(states.shape, states.dtype),
-        in_specs=[vmem, smem, smem, vmem, anywhere, anywhere, anywhere],
+        in_specs=[anywhere] * 7,
         out_specs=vmem,
         scratch_shapes=[
+            pltpu.VMEM(states.shape, BF16),
+            pltpu.SMEM(step_index.shape, jnp.int32),
+            pltpu.SMEM(plan.shape, jnp.int32),
+            pltpu.VMEM(time_weight.shape, BF16),
             pltpu.VMEM((MOD, width), BF16),
             pltpu.VMEM((hidden, width), BF16),
             pltpu.VMEM((hidden, width), BF16),
@@ -380,10 +395,8 @@
             pltpu.VMEM((N, 8, LANES), F32),
             pltpu.VMEM((N, 8, LANES), F32),
             pltpu.VMEM((16, width), BF16),
-            pltpu.VMEM((16, LANES), F32),
-            pltpu.VMEM((16, LANES), F32),
-            pltpu.VMEM((N, 16, LANES), F32),
-            pltpu.VMEM((N, 16, LANES), F32),
+            pltpu.VMEM((1, 2, LANES), F32),
+            pltpu.VMEM((64, 2, LANES), F32),
             pltpu.VMEM((16, width), BF16),
             pltpu.VMEM((8, hidden), F32),
             pltpu.VMEM(block, F32),
@@ -400,13 +413,16 @@
             pltpu.VMEM(block, F32),
             pltpu.VMEM(block, BF16),
             pltpu.VMEM(block, BF16),
-            dma((3,)), dma((4,)), dma((4,)), dma((1,)), dma((64,)),
-            dma((1,)), dma((4, 4, 4)), dma((1,)), dma((1,)), dma((1,)), dma((1,)),
+            pltpu.VMEM((CHUNKS, LANES), F32),
+            pltpu.VMEM((CHUNKS, LANES), F32),
+            dma((7,)), dma((3,)), dma((3,)), dma((1,)), dma((64,)),
+            dma((1,)), dma((4, 4, 4)), dma((1,)), dma((1,)), dma((2,)), dma((2,)),
+            pltpu.SemaphoreType.REGULAR,
         ],
         name="denoise",
         cost_estimate=pl.CostEstimate(flops=800_000_000, bytes_accessed=3_300_000, transcendentals=100_000),
         compiler_params=pltpu.CompilerParams(
-            collective_id=0, has_side_effects=True, vmem_limit_bytes=40 * 1024 * 1024
+            collective_id=0, has_side_effects=True, vmem_limit_bytes=60 * 1024 * 1024
         ),
     )(states, step_index, plan, time_weight, mod_weight, up_weight, down_weight)
 

time: 71.9 us -> 66.4 us (0.924)
  local copies, waits for them, and re-layouts: 6.51 us -> 1.42 us
    unnamed x13 -> x1, local copies, waits for them, and re-layouts: 6.51 us -> 1.42 us
where the time goes in v2:
time: 66.4 us; the launch traced here: 66.3 us
  Pallas kernels  64.2 us (97%)
  local copies, waits for them, and re-layouts  1.42 us (2%)
    pallas_call x1, Pallas kernels, local(): pl.pallas_call(kernel, out_shape=jax.ShapeDtypeStruct(states.shape, state...  64.2 us
    unnamed x1, local copies, waits for them, and re-layouts  1.42 us

profile of v2, /device:TPU:1, one launch (start us, length us, event | category | flops | bytes accessed | tf_op | source)
XLA Modules:
  0.0 66.3 jit_solution(12350051090034020729)
XLA Ops:
  0.7 64.2 %denoise.1 = bf16[1,5,3072]{2,1,0:T(8,128)(2,1)} custom-call(bf16[1,5,3072]{2,1,0:T(8,128)(2,1)} %states_hbm.1, s32[1]{0:T(128)S(6)} %copy.9.step_hbm, s32[29]{0:T(128)} %plan_hbm.1, bf16[48,256]{1,0:T(8,128)(2,1)} %time_hbm.1, bf16[1,144,3072]{2,1,0:T(8,128)(2,1)} %mod_hbm.1, bf16[1,192,3072]{2,1,0:T(8,128)(2,1)} %up_hbm.1, bf16[1,192,3072]{2,1,0:T(8,128)(2,1)} %down_hbm.1), custom_call_target="tpu_custom_call" | custom-call | flops 800000000 | bytes 3300000 | tf_op jit(solution)/shard_map/denoise/pallas_call | solution.py:379
  64.8 1.4 %copy.10 = bf16[1,5,3072]{2,1,0:T(8,128)(2,1)} copy(bf16[1,5,3072]{2,1,0:T(8,128)(2,1)} %denoise.1) | data formatting | bytes 61440

commit v3 on v2

--- a/solution.py
+++ b/solution.py
@@ -16,7 +16,7 @@
 TOK = 5
 CHUNKS = 24
 USED = TOK * CHUNKS
-ROWS = 128
+ROWS = 120
 PER = 48
 MOD = 144
 EVERYONE = sorted(
@@ -95,16 +95,13 @@
     center = rows - jnp.mean(rows, axis=-1, keepdims=True)
     spread = jnp.mean(center * center, axis=-1, keepdims=True)
     normed = center * lax.rsqrt(spread + 1e-06)
-    own_f32[USED:ROWS, :] = jnp.zeros((ROWS - USED, LANES), F32)
-    raw_pack[USED:ROWS, :] = jnp.zeros((ROWS - USED, LANES), F32)
-    gate_pack[USED:ROWS, :] = jnp.zeros((ROWS - USED, LANES), F32)
     for c in range(CHUNKS):
         own_f32[TOK * c : TOK * c + TOK, :] = normed[:, c * LANES : (c + 1) * LANES]
         raw_pack[TOK * c : TOK * c + TOK, :] = rows[:, c * LANES : (c + 1) * LANES]
     own[...] = own_f32[...].astype(BF16)
     own_rows[...] = raw_pack[...].astype(BF16)
-    for i in range(8):
-        pack[i, USED:ROWS, :] = jnp.zeros((ROWS - USED, LANES), F32)
+    for i in range(4):
+        unpack[i, ROWS:, :] = jnp.zeros((8, LANES), F32)
 
     pl.semaphore_wait(barrier, 16)
     pl.semaphore_signal(ready, inc=1, device_id={"section": prev_section}, device_id_type=MESH)
@@ -134,15 +131,6 @@
 
     rows_copy = pass_on(own_rows, rows_in, s_send.at[0], s_recv.at[0], seq)
     rows_copy.start()
-
-    wait(cond_y.at[0:7], small_recv.at[0])
-    total = cond_y[0]
-    for i in range(1, N):
-        total = total + cond_y[i]
-    cond_stage[1] = total
-    cond_z[z] = total
-    for k in far_first:
-        send(cond_stage.at[1], cond_z.at[z], small_send.at[1], small_recv.at[1], ring_z[k])
 
     up_z, down_z = at(y, plus(z, 1)), at(y, plus(z, -1))
     up_y, down_y = at(plus(y, 1), z), at(plus(y, -1), z)
@@ -163,7 +151,7 @@
     def unpack_slab(offset, odd_class):
         s = slab(offset, odd_class)
         for j in range(4):
-            unpack[j] = gathered[source(odd_class, offset, j)].astype(F32)
+            unpack[j, 0:ROWS, :] = gathered[source(odd_class, offset, j)].astype(F32)
         for pair in range(2):
             for c in range(CHUNKS):
                 both = jnp.concatenate(
@@ -187,9 +175,32 @@
             forward(src, up)
             forward(src, down)
 
-    unpack_slab(0, 0)
-    unpack_slab(0, 1)
-
+    wait(cond_y.at[0:7], small_recv.at[0])
+    total = cond_y[0]
+    for i in range(1, N):
+        total = total + cond_y[i]
+    cond_stage[1] = total
+    cond_z[z] = total
+    for k in far_first:
+        send(cond_stage.at[1], cond_z.at[z], small_send.at[1], small_recv.at[1], ring_z[k])
+
+    def gather_step(h):
+        for j in range(4):
+            for odd_class in (0, 1):
+                up, down = (up_y, down_y) if odd_class else (up_z, down_z)
+                src = arrive(-h, odd_class, j)
+                if h < 3 or j < 2:
+                    forward(src, up)
+                src = arrive(h, odd_class, j)
+                if h < 3 or j >= 2:
+                    forward(src, down)
+
+    def unpack_step(h):
+        for odd_class in (0, 1):
+            unpack_slab(h, odd_class)
+            unpack_slab(-h, odd_class)
+
+    gather_step(1)
     wait(cond_z.at[0:7], small_recv.at[1])
     for zz in range(N):
         for m in range(3):
@@ -209,34 +220,14 @@
     for dy, dz in EVERYONE:
         send(mod_stage.at[0], mod_all.at[seq], small_send.at[2], small_recv.at[2], at(plus(y, dy), plus(z, dz)))
 
-    def gather_step(h):
-        for j in range(4):
-            for odd_class in (0, 1):
-                up, down = (up_y, down_y) if odd_class else (up_z, down_z)
-                src = arrive(-h, odd_class, j)
-                if h < 3 or j < 2:
-                    forward(src, up)
-                src = arrive(h, odd_class, j)
-                if h < 3 or j >= 2:
-                    forward(src, down)
-
-    def unpack_step(h):
-        for odd_class in (0, 1):
-            unpack_slab(h, odd_class)
-            unpack_slab(-h, odd_class)
-
-    gather_step(1)
+    unpack_slab(0, 0)
+    unpack_slab(0, 1)
+    gather_step(2)
+
     unpack_step(1)
-    gather_step(2)
-
+    gather_step(3)
     unpack_step(2)
-    gather_step(3)
     unpack_step(3)
-    for j in range(4):
-        for odd_class in (0, 1):
-            arrive(4, odd_class, j)
-    unpack_slab(4, 0)
-    unpack_slab(4, 1)
 
     wait(mod_all.at[0:63], small_recv.at[2])
 
@@ -267,6 +258,12 @@
         gate_out[c : c + 1, :] = modulation(2 * CHUNKS + c)
     gate_copy = pass_on(gate_out, gate_in, s_send.at[1], s_recv.at[1], seq)
     gate_copy.start()
+
+    for j in range(4):
+        for odd_class in (0, 1):
+            arrive(4, odd_class, j)
+    unpack_slab(4, 0)
+    unpack_slab(4, 1)
 
     def compute(first_slab, count):
         m = count * 32
@@ -402,7 +399,7 @@
             pltpu.VMEM(block, F32),
             pltpu.VMEM(block, BF16),
             pltpu.VMEM((64,) + block, BF16),
-            pltpu.VMEM((4,) + block, F32),
+            pltpu.VMEM((4, ROWS + 8, LANES), F32),
             pltpu.VMEM((16, 32, width), BF16),
             pltpu.VMEM((16, 4) + block, BF16),
             pltpu.VMEM((8,) + block, F32),

time: 66.4 us -> 63.7 us (0.959)
  Pallas kernels: 64.2 us -> 61.4 us
    pallas_call x1, Pallas kernels: 64.2 us -> 61.4 us  [local(): pl.pallas_call(kernel, out_shape=jax.ShapeDtypeStruct(states.shape, state...]
where the time goes in v3:
time: 63.7 us; the launch traced here: 63.5 us
  Pallas kernels  61.4 us (96%)
  local copies, waits for them, and re-layouts  1.42 us (2%)
  between operations  0.66 us (1%)
    pallas_call x1, Pallas kernels, local(): pl.pallas_call(kernel, out_shape=jax.ShapeDtypeStruct(states.shape, state...  61.4 us
    unnamed x1, local copies, waits for them, and re-layouts  1.42 us

profile of v3, /device:TPU:1, one launch (start us, length us, event | category | flops | bytes accessed | tf_op | source)
XLA Modules:
  0.0 63.5 jit_solution(14697884603987305677)
XLA Ops:
  0.7 61.4 %denoise.1 = bf16[1,5,3072]{2,1,0:T(8,128)(2,1)} custom-call(bf16[1,5,3072]{2,1,0:T(8,128)(2,1)} %states_hbm.1, s32[1]{0:T(128)S(6)} %copy.9.step_hbm, s32[29]{0:T(128)} %plan_hbm.1, bf16[48,256]{1,0:T(8,128)(2,1)} %time_hbm.1, bf16[1,144,3072]{2,1,0:T(8,128)(2,1)} %mod_hbm.1, bf16[1,192,3072]{2,1,0:T(8,128)(2,1)} %up_hbm.1, bf16[1,192,3072]{2,1,0:T(8,128)(2,1)} %down_hbm.1), custom_call_target="tpu_custom_call" | custom-call | flops 800000000 | bytes 3300000 | tf_op jit(solution)/shard_map/denoise/pallas_call | solution.py:376
  62.1 1.4 %copy.10 = bf16[1,5,3072]{2,1,0:T(8,128)(2,1)} copy(bf16[1,5,3072]{2,1,0:T(8,128)(2,1)} %denoise.1) | data formatting | bytes 61440

commit v4 on v3

--- a/solution.py
+++ b/solution.py
@@ -129,8 +129,6 @@
     for k in far_first:
         send(own, gathered.at[seq], g_send.at[0], g_recv.at[seq], ring_y[k] + odd * (ring_z[k] - ring_y[k]))
 
-    rows_copy = pass_on(own_rows, rows_in, s_send.at[0], s_recv.at[0], seq)
-    rows_copy.start()
 
     up_z, down_z = at(y, plus(z, 1)), at(y, plus(z, -1))
     up_y, down_y = at(plus(y, 1), z), at(plus(y, -1), z)
@@ -191,8 +189,8 @@
                 src = arrive(-h, odd_class, j)
                 if h < 3 or j < 2:
                     forward(src, up)
-                src = arrive(h, odd_class, j)
-                if h < 3 or j >= 2:
+                src = arrive(h, odd_class, 3 - j)
+                if h < 3 or j < 2:
                     forward(src, down)
 
     def unpack_step(h):
@@ -226,6 +224,8 @@
 
     unpack_step(1)
     gather_step(3)
+    rows_copy = pass_on(own_rows, rows_in, s_send.at[0], s_recv.at[0], seq)
+    rows_copy.start()
     unpack_step(2)
     unpack_step(3)
 

time: 63.7 us -> 63 us (0.989)
  Pallas kernels: 61.4 us -> 60.7 us
    pallas_call x1, Pallas kernels: 61.4 us -> 60.7 us  [local(): pl.pallas_call(kernel, out_shape=jax.ShapeDtypeStruct(states.shape, state...]
where the time goes in v4:
time: 63 us; the launch traced here: 62.8 us
  Pallas kernels  60.7 us (96%)
  local copies, waits for them, and re-layouts  1.42 us (2%)
  between operations  0.66 us (1%)
    pallas_call x1, Pallas kernels, local(): pl.pallas_call(kernel, out_shape=jax.ShapeDtypeStruct(states.shape, state...  60.7 us
    unnamed x1, local copies, waits for them, and re-layouts  1.42 us

profile of v4, /device:TPU:1, one launch (start us, length us, event | category | flops | bytes accessed | tf_op | source)
XLA Modules:
  0.0 62.8 jit_solution(7526893081100279822)
XLA Ops:
  0.7 60.7 %denoise.1 = bf16[1,5,3072]{2,1,0:T(8,128)(2,1)} custom-call(bf16[1,5,3072]{2,1,0:T(8,128)(2,1)} %states_hbm.1, s32[1]{0:T(128)S(6)} %copy.9.step_hbm, s32[29]{0:T(128)} %plan_hbm.1, bf16[48,256]{1,0:T(8,128)(2,1)} %time_hbm.1, bf16[1,144,3072]{2,1,0:T(8,128)(2,1)} %mod_hbm.1, bf16[1,192,3072]{2,1,0:T(8,128)(2,1)} %up_hbm.1, bf16[1,192,3072]{2,1,0:T(8,128)(2,1)} %down_hbm.1), custom_call_target="tpu_custom_call" | custom-call | flops 800000000 | bytes 3300000 | tf_op jit(solution)/shard_map/denoise/pallas_call | solution.py:376
  61.4 1.4 %copy.10 = bf16[1,5,3072]{2,1,0:T(8,128)(2,1)} copy(bf16[1,5,3072]{2,1,0:T(8,128)(2,1)} %denoise.1) | data formatting | bytes 61440
